TPU v7x, 32 devices: a whole 2x2x4 slice. The times are simulated.
32 devices in a mesh: grp: 2 (over y), seq: 4 (over z), wt: 2 (over x), head: 2 (over core).
Axes of the slice: x: 2, y: 2, z: 4, core: 2. Of those that a mesh axis runs over, the one named last changes fastest.
Arguments:
- hidden: bfloat16 [2048, 2048], P(('grp', 'seq', 'wt'), 'head'), parts along dimension 0, may hold values from -6 to 6
- norm_gain: float32 [2048], replicated, may hold values from 0.1 to 1.9
- w_proj_x: bfloat16 [2048, 4096], P('wt', 'head'), may hold values from -0.125 to 0.125
- w_proj_bc: bfloat16 [2048, 512], P('wt', 'head'), may hold values from -0.125 to 0.125
- w_proj_dt: bfloat16 [2048, 32], P('wt', 'head'), may hold values from -0.125 to 0.125
- dt_bias: float32 [32], P('head'), may hold values from -4 to -1
- a_log: float32 [32], P('head'), may hold values from -20 to 1
- d_skip: float32 [32], P('head'), may hold values from 0.5 to 1.5
- inner_gain: float32 [4096], P('head'), may hold values from 0.1 to 1.9
- w_out: bfloat16 [4096, 2048], P('head', 'wt'), may hold values from -0.09375 to 0.09375
- lengths: int32 [16], P(('grp', 'seq', 'wt')), parts along dimension 0, may hold values from 1 to 128, 768 in all
- mix_index: int32 [16, 4], P(('grp', 'seq', 'wt')), parts along dimension 0, may hold values from 0 to 7, as said below
- mix_gain: float32 [16, 4], P(('grp', 'seq', 'wt')), parts along dimension 0, may hold values from -0.5 to 0.5
Outputs:
- layer_out: bfloat16 [2048, 2048], P(('grp', 'seq', 'wt'), 'head'), parts along dimension 0
There are 2 independent parts, one for each index of `grp`. A program takes and returns all parts, laid end to end along the dimension named above; an argument that names none is the same for every part. Nothing has to cross between parts.
Inputs may be any that keep to these rules, and one draw needn't show every extreme that they name: `mix_index`: each listed block belongs to the same shard of 128 positions as its row's block or to one of the two shards next to it.
All inputs are finite; a program needn't handle non-finite values. No bound on the sum of `lengths` on one device may be relied on, other than what follows from the above.
Results may differ from a plain program's by a relative error of at most 0.0065.
Values may be sent and summed in bfloat16 or wider, within the bound.
A program may use at most 320 MiB of HBM per device.

v0:
```python
import jax
import jax.numpy as jnp
from jax import lax
from jax.sharding import PartitionSpec as P

SPAN = 128
BLK = 128
eps_value = 1e-05
highest = lax.Precision.HIGHEST


def prefix(value, axis, join, neutral):
    count, mine = (lax.axis_size(axis), lax.axis_index(axis))
    pieces = jax.tree.map(lambda part: lax.all_gather(part, axis), value)
    total = jax.tree.map(
        lambda part, zero: jnp.full_like(part, 0) + jnp.asarray(zero, part.dtype), value, neutral
    )

    def turn(position, total):
        longer = join(total, jax.tree.map(lambda part: part[position], pieces))
        return jax.tree.map(lambda new, old: jnp.where(position < mine, new, old), longer, total)

    return lax.fori_loop(0, count - 1, turn, total)


def extended(cells, sides, width):
    for axis, dim in sides:
        count = lax.axis_size(axis)
        ends = count - 1
        head = lax.slice_in_dim(cells, 0, width, axis=dim)
        tail = lax.slice_in_dim(cells, cells.shape[dim] - width, cells.shape[dim], axis=dim)
        cells = jnp.concatenate(
            [
                lax.ppermute(tail, axis, [(i, (i + 1) % count) for i in range(ends)]),
                cells,
                lax.ppermute(head, axis, [((i + 1) % count, i) for i in range(ends)]),
            ],
            axis=dim,
        )
    return cells


def span_local(x_span, b_span, c_span, dt_span, log_span):
    cumulated = jnp.cumsum(log_span, axis=0)
    length = x_span.shape[0]
    rows_at = jnp.arange(length, dtype=jnp.int32)
    lower_part = rows_at[:, None] >= rows_at[None, :]
    difference = cumulated.T[:, :, None] - cumulated.T[:, None, :]
    decays = jnp.where(lower_part[None], jnp.exp(jnp.where(lower_part[None], difference, 0.0)), 0.0)
    scores = jnp.dot(c_span, b_span.T, precision=highest)
    weights = scores[None] * decays * dt_span.T[:, None, :]
    outputs = jnp.einsum("hts,shp->thp", weights, x_span, precision=highest)
    tail_decay = jnp.exp(cumulated[-1][None, :] - cumulated) * dt_span
    weighted_x = x_span * tail_decay[:, :, None]
    state_new = jnp.einsum("shp,sn->hpn", weighted_x, b_span, precision=highest)
    return (outputs, state_new, cumulated)


def from_state(c_span, cumulated, state_in):
    return (
        jnp.einsum("tn,hpn->thp", c_span, state_in, precision=highest)
        * jnp.exp(cumulated)[:, :, None]
    )


def combine(earlier, later):
    return (earlier[0] + later[0], jnp.exp(later[0])[:, None, None] * earlier[1] + later[1])


def body(
    hidden,
    norm_gain,
    w_proj_x,
    w_proj_bc,
    w_proj_dt,
    dt_bias,
    a_log,
    d_skip,
    inner_gain,
    w_out,
    lengths,
    mix_index,
    mix_gain,
):
    tokens_here = hidden.shape[0]
    half_width = hidden.shape[1]
    whole_input = lax.all_gather(hidden, "head", axis=1, tiled=True)
    floats = whole_input.astype(jnp.float32)
    normed = (
        floats
        * lax.rsqrt(jnp.mean(floats * floats, axis=-1, keepdims=True) + eps_value)
        * norm_gain
    ).astype(jnp.bfloat16)
    pieces = (
        lax.all_gather(w_proj_x, "wt", axis=0, tiled=True),
        lax.all_gather(w_proj_bc, "wt", axis=0, tiled=True),
        lax.all_gather(w_proj_dt, "wt", axis=0, tiled=True),
    )
    x_sum, bc_sum, dt_raw = tuple(
        (
            jnp.dot(normed, weight_piece, preferred_element_type=jnp.float32)
            for weight_piece in pieces
        )
    )
    heads_here = w_proj_dt.shape[1]
    state_size = w_proj_bc.shape[1] // 2
    head_size = w_proj_x.shape[1] // heads_here
    x_in = jax.nn.silu(x_sum).astype(jnp.bfloat16)
    bc_in = jax.nn.silu(bc_sum).astype(jnp.bfloat16)
    shard_at = lax.axis_index(("seq", "wt"))
    live_mask = (jnp.arange(tokens_here, dtype=jnp.int32) < lengths[0]).astype(jnp.float32)
    steps_dt = jax.nn.softplus(dt_raw + dt_bias) * live_mask[:, None]
    log_decay = -steps_dt * jnp.exp(a_log)
    spans = tokens_here // SPAN
    x_float = x_in.astype(jnp.float32).reshape(spans, SPAN, heads_here, head_size)
    b_float = bc_in[:, :state_size].astype(jnp.float32).reshape(spans, SPAN, state_size)
    c_float = bc_in[:, state_size:].astype(jnp.float32).reshape(spans, SPAN, state_size)
    dt_float = steps_dt.reshape(spans, SPAN, heads_here)
    log_float = log_decay.reshape(spans, SPAN, heads_here)
    outputs, fresh_states, cumulated = jax.vmap(span_local)(
        x_float, b_float, c_float, dt_float, log_float
    )
    running = jnp.zeros((heads_here, head_size, state_size), jnp.float32)
    before = jnp.zeros((heads_here,), jnp.float32)
    arriving = [running]
    decayed = [before]
    running = jnp.exp(cumulated[0, -1])[:, None, None] * running + fresh_states[0]
    before = cumulated[0, -1]
    identity_pair = (
        jnp.zeros((heads_here,), jnp.float32),
        jnp.zeros((heads_here, head_size, state_size), jnp.float32),
    )
    entering = prefix((before, running), ("seq", "wt"), combine, identity_pair)
    initial = entering[1]
    incoming = jnp.stack(arriving) + jnp.exp(jnp.stack(decayed))[:, :, None, None] * initial[None]
    outputs = outputs + jax.vmap(from_state)(c_float, cumulated, incoming)
    y_full = outputs.reshape(tokens_here, heads_here, head_size) + d_skip[
        None, :, None
    ] * x_float.reshape(tokens_here, heads_here, head_size)
    scaling = lax.rsqrt(jnp.mean(y_full * y_full, axis=-1, keepdims=True) + eps_value)
    y_norm = (
        (y_full * scaling * inner_gain.reshape(heads_here, head_size))
        .astype(jnp.bfloat16)
        .reshape(tokens_here, heads_here * head_size)
    )
    partial_out = jnp.dot(
        y_norm, lax.all_gather(w_out, "wt", axis=1, tiled=True), preferred_element_type=jnp.float32
    )
    head_total = lax.psum_scatter(partial_out, "head", scatter_dimension=1, tiled=True)
    own_part = hidden.astype(jnp.float32)
    mixed_in = (own_part + head_total).astype(jnp.bfloat16)
    widened = extended(mixed_in, ((("seq", "wt"), 0),), tokens_here)
    per_shard = tokens_here // BLK
    blocks = widened.reshape(3 * per_shard, BLK, half_width)
    relative = mix_index - (shard_at * per_shard - per_shard)
    summed_mix = mixed_in.astype(jnp.float32).reshape(per_shard, BLK, half_width)
    for member in range(mix_index.shape[1]):
        summed_mix = summed_mix + mix_gain[:, member][:, None, None] * jnp.take(
            blocks, relative[:, member], axis=0
        ).astype(jnp.float32)
    return summed_mix.reshape(tokens_here, half_width).astype(jnp.bfloat16)


def solution(mesh):
    in_specs = (
        P(("grp", "seq", "wt"), "head"),
        P(),
        P("wt", "head"),
        P("wt", "head"),
        P("wt", "head"),
        P("head"),
        P("head"),
        P("head"),
        P("head"),
        P("head", "wt"),
        P(("grp", "seq", "wt")),
        P(("grp", "seq", "wt"), None),
        P(("grp", "seq", "wt"), None),
    )
    out_specs = P(("grp", "seq", "wt"), "head")
    return jax.shard_map(body, mesh=mesh, in_specs=in_specs, out_specs=out_specs, check_vma=False)
```

profile of v0, /device:TPU:9, one launch (start us, length us, event | category | flops | bytes accessed | tf_op | source)
XLA Modules:
  0.0 417.1 jit_solution(728118675776157198)
XLA Ops:
  6.5 0.7 all-gather.9.cloned.1.call-update
  7.3 0.0 all-gather.7.cloned.1.call-start
  7.3 0.7 all-gather.7.cloned.1.call-update
  8.0 0.0 all-gather.13.cloned.1.call-start
  8.7 0.7 exp.58
  9.4 3.6 all_gather.25
  13.0 3.8 all_gather.22
  16.8 0.2 fusion.3
  17.0 1.0 fusion.39
  18.1 0.1 multiply_bitcast_fusion
  18.2 0.1 copy.23
  18.3 0.2 reduce_window_sum.13
  18.4 0.1 copy.27
  18.5 0.1 bitcast_exponential_fusion
  18.6 0.1 copy.28
  18.7 12.7 %all-gather.9.cloned.1.call-done = bf16[2048,256]{1,0:T(8,128)(2,1)} async-done(((bf16[1024,256]{1,0:T(8,128)(2,1)}), bf16[2048,256]{1,0:T(8,128)(2,1)}) %all-gather.9.cloned.1.call-update) | async-done | bytes 1048592 | tf_op jit(solution)/shard_map/all_gather | solution.py:96
  31.4 1.6 multiply_convert_fusion.1
  33.0 104.0 %all-gather.7.cloned.1.call-done = bf16[2048,2048]{1,0:T(8,128)(2,1)} async-done(((bf16[1024,2048]{1,0:T(8,128)(2,1)}), bf16[2048,2048]{1,0:T(8,128)(2,1)}) %all-gather.7.cloned.1.call-update) | async-done | bytes 8388624 | tf_op jit(solution)/shard_map/all_gather | solution.py:95
  137.0 0.3 mul.233
  137.3 5.3 %bitcast_multiply_fusion.1 = (f32[128,2048]{1,0:T(8,128)S(1)}, bf16[128,2048]{1,0:T(8,128)(2,1)S(1)}) fusion(f32[16,8,16,128]{3,2,1,0:T(8,128)S(1)} %bitcast.107, bf16[2048,2048]{1,0:T(8,128)(2,1)} %all-gather.7.cloned.1.call-done, bf16[128,2048]{1,0:T(8,128)(2,1)S(1)} %all_gather.22, f32[2048]{0:T(1024)S(1)} %copy-done.4, f32[128]{0:T(128)S(1)} %add_rsqrt_fusion.1), kind=kOutput, calls=%fused_computation.17 | convolution fusion | flops 1076625408 | bytes 11543040 | tf_op jit(solution)/shard_map/dot_general | solution.py:101
  142.6 0.0 copy-start.3
  142.6 0.3 copy.34
  142.9 1.6 convolution_add_fusion
  144.5 0.0 all-gather.13.cloned.1.call-update
  144.6 0.0 all-gather.11.cloned.1.call-start
  144.6 0.5 all-gather.11.cloned.1.call-update
  145.1 0.0 reduce-scatter.2.cloned.1.call-start
  145.2 0.1 copy.24
  145.3 13.8 %all-gather = f32[8,1,16]{2,1,0:T(1,128)S(1)} all-gather(f32[1,1,16]{2,1,0:T(1,128)S(1)} %get-tuple-element.141), channel_id=2, replica_groups=mesh['grp'=2,'seq'=4,'wt'=2,'head'=2] {'seq','wt'}, dimensions={0}, use_global_device_ids=true | all-gather | bytes 576 | tf_op jit(solution)/shard_map/all_gather | solution.py:14
  159.1 0.1 broadcast_bitcast_fusion
  159.2 0.1 fusion.35
  159.3 0.2 copy.36
  159.5 0.3 copy.33
  159.8 107.6 %all-gather.13.cloned.1.call-done = f32[128,128,128]{2,1,0:T(8,128)} async-done(((f32[16,128,128]{2,1,0:T(8,128)}), f32[128,128,128]{2,1,0:T(8,128)}) %all-gather.13.cloned.1.call-update) | async-done | bytes 8388624 | tf_op jit(solution)/shard_map/all_gather | solution.py:14
  267.4 10.8 %while.15 = (s32[]{:T(128)}, f32[16,128,128]{2,1,0:T(8,128)S(1)}, s32[]{:T(128)}, f32[8,16]{1,0:T(8,128)S(1)}, f32[8,16,128,128]{3,2,1,0:T(8,128)}, /*index=5*/s32[]{:T(128)}, s32[]{:T(128)}) while((s32[]{:T(128)}, f32[16,128,128]{2,1,0:T(8,128)S(1)}, s32[]{:T(128)}, f32[8,16]{1,0:T(8,128)S(1)}, f32[8,16,128,128]{3,2,1,0:T(8,128)}, ...), condition=%wide.region_3.4_spmd.clone, body=%wide.region_2.3_spmd.clone.sunk | while | flops 1048580 | bytes 3146025 | solution.py:23
  267.4 1.5 fusion.62
  268.9 1.5 fusion.62
  270.4 1.5 fusion.62
  271.9 1.5 fusion.62
  273.4 1.5 fusion.62
  274.9 1.6 fusion.62
  276.6 1.6 fusion.62
  278.2 0.0 copy-start.1
  278.2 0.6 fusion.1
  278.8 2.6 fusion.9
  281.4 0.1 copy.32
  281.5 1.7 copy.35
  283.2 90.1 %all-gather.11.cloned.1.call-done = bf16[2048,2048]{1,0:T(8,128)(2,1)} async-done(((bf16[2048,1024]{1,0:T(8,128)(2,1)}), bf16[2048,2048]{1,0:T(8,128)(2,1)}) %all-gather.11.cloned.1.call-update) | async-done | bytes 8388624 | tf_op jit(solution)/shard_map/all_gather | solution.py:147
  373.3 0.3 mul.247
  373.6 0.0 copy-start
  373.6 0.0 copy-start.5
  373.7 0.0 copy-start.2
  373.7 6.1 %fusion.16 = f32[128,2048]{1,0:T(8,128)} fusion(bf16[2048,2048]{1,0:T(8,128)(2,1)} %all-gather.11.cloned.1.call-done, f32[16,8,16,128]{3,2,1,0:T(8,128)S(1)} %bitcast.101, f32[128,2048]{1,0:T(8,128)S(1)} %copy.35, f32[2048]{0:T(1024)S(1)} %copy-done.1, f32[2048]{0:T(1024)S(1)} %broadcast_bitcast_fusion, bf16[128,2048]{1,0:T(8,128)(2,1)S(1)} %get-tuple-element.153), kind=kOutput, calls=%fused_computation.29 | convolution fusion | flops 1075314688 | bytes 12075008 | tf_op jit(solution)/shard_map/dot_general | solution.py:146
  379.8 0.0 reduce-scatter.2.cloned.1.call-update
  379.8 9.4 %reduce-scatter.2.cloned.1.call-done = f32[128,1024]{1,0:T(8,128)} async-done(((f32[128,2048]{1,0:T(8,128)}), f32[128,1024]{1,0:T(8,128)}) %reduce-scatter.2.cloned.1.call-update) | async-done | bytes 524304 | tf_op jit(solution)/shard_map/reduce_scatter | solution.py:149
  389.2 1.1 add_convert_fusion
  390.3 3.1 collective-permute-start
  393.4 3.1 collective-permute-start.1
  396.5 0.6 fusion.53
  404.6 0.7 fusion.52
  405.2 0.0 collective-permute-done
  405.2 1.7 collective-permute-done.1
  407.0 0.1 pad_maximum_fusion
  407.0 3.6 fusion.31
  (23 shorter events, 0.1 us)
Async XLA Ops:
  6.5 130.8 %copy-start.4 = (f32[2048]{0:T(1024)S(1)}, f32[2048]{0:T(1024)}, u32[]{:S(2)}) copy-start(f32[2048]{0:T(1024)} %param.18) | copy-start | bytes 24580
  6.5 24.9 %all-gather.9.cloned.1.call-start = ((), (), s32[]{:S(2)}) async-start(), calls=%async_computation.2 | async-start | bytes 1572864 | tf_op jit(solution)/shard_map/all_gather | solution.py:96
  7.3 129.7 %all-gather.7.cloned.1.call-start = ((), (), s32[]{:S(2)}) async-start(), calls=%async_computation.1 | async-start | bytes 12582912 | tf_op jit(solution)/shard_map/all_gather | solution.py:95
  8.0 259.4 %all-gather.13.cloned.1.call-start = ((), (), s32[]{:S(2)}) async-start(), calls=%async_computation.5 | async-start | bytes 9437184 | tf_op jit(solution)/shard_map/all_gather | solution.py:14
  142.6 16.5 %copy-start.3 = (f32[16]{0:T(128)S(1)}, f32[16]{0:T(128)}, u32[]{:S(2)}) copy-start(f32[16]{0:T(128)} %param.24) | copy-start | bytes 196
  144.6 228.7 %all-gather.11.cloned.1.call-start = ((), (), s32[]{:S(2)}) async-start(), calls=%async_computation.3 | async-start | bytes 12582912 | tf_op jit(solution)/shard_map/all_gather | solution.py:147
  145.1 244.1 %reduce-scatter.2.cloned.1.call-start = ((), (), s32[]{:S(2)}) async-start(), calls=%async_computation.4 | async-start | bytes 1572864 | tf_op jit(solution)/shard_map/reduce_scatter | solution.py:149
  278.2 95.4 %copy-start.1 = (f32[2048]{0:T(1024)S(1)}, f32[2048]{0:T(1024)}, u32[]{:S(2)}) copy-start(f32[2048]{0:T(1024)} %param.25) | copy-start | bytes 24580
  373.6 15.6 %copy-start = (bf16[128,1024]{1,0:T(8,128)(2,1)S(1)}, bf16[128,1024]{1,0:T(8,128)(2,1)}, u32[]{:S(2)}) copy-start(bf16[128,1024]{1,0:T(8,128)(2,1)} %param.17) | copy-start | bytes 786436
  373.6 22.9 %copy-start.5 = (s32[1,4]{1,0:T(1,128)S(1)}, s32[1,4]{1,0:T(1,128)}, u32[]{:S(2)}) copy-start(s32[1,4]{1,0:T(1,128)} %param.28) | copy-start | bytes 52
  373.7 30.9 %copy-start.2 = (f32[1,4]{1,0:T(1,128)S(1)}, f32[1,4]{1,0:T(1,128)}, u32[]{:S(2)}) copy-start(f32[1,4]{1,0:T(1,128)} %param.29) | copy-start | bytes 52
  390.3 14.9 %collective-permute-start = (bf16[128,1024]{1,0:T(8,128)(2,1)S(1)}, bf16[128,1024]{1,0:T(8,128)(2,1)S(1)}, u32[]{:S(2)}, u32[]{:S(2)}) collective-permute-start(bf16[128,1024]{1,0:T(8,128)(2,1)S(1)} %add_convert_fusion), channel_id=1, source_target_pairs={{0,2},{2,4},{4,6},{6,8},{8,10},{10,12},{12,14},{1,3},{3,5},{5,7},{... | collective-permute-start | bytes 786440 | tf_op jit(solution)/shard_map/ppermute | solution.py:34
  393.4 13.5 %collective-permute-start.1 = (bf16[128,1024]{1,0:T(8,128)(2,1)S(1)}, bf16[128,1024]{1,0:T(8,128)(2,1)S(1)}, u32[]{:S(2)}, u32[]{:S(2)}) collective-permute-start(bf16[128,1024]{1,0:T(8,128)(2,1)S(1)} %add_convert_fusion), channel_id=1, source_target_pairs={{2,0},{4,2},{6,4},{8,6},{10,8},{12,10},{14,12},{3,1},{5,3},{7,5},{... | collective-permute-start | bytes 786440 | tf_op jit(solution)/shard_map/ppermute | solution.py:36
Sparse Core Ops, SparseCore 0:
  8.9 22.4 all-gather.8
  32.9 103.9 all-gather.6
  144.7 122.6 all-gather.12
  268.8 104.4 all-gather.10
  379.9 9.2 reduce-scatter.1
where the time goes:
time: 418 us; the launch traced here: 417 us
  waiting for transfers between devices  327 us (78%)
  between operations  21.4 us (5%)
  blocking collectives  21.3 us (5%)
  matrix products  18.9 us (5%)
  other arithmetic  15.8 us (4%)
  starting transfers between devices  6.34 us (2%)
  local copies, waits for them, and re-layouts  5.7 us (1%)
    all_gather x1, waiting for transfers between devices, prefix(): pieces = jax.tree.map(lambda part: lax.all_gather(part, axis), value)  108 us
    all_gather x1, waiting for transfers between devices, body(): lax.all_gather(w_proj_x, 'wt', axis=0, tiled=True)  104 us
    all_gather x1, waiting for transfers between devices, body(): lax.all_gather(w_out, 'wt', axis=1, tiled=True)  90.1 us
    all_gather x1, blocking collectives, prefix(): pieces = jax.tree.map(lambda part: lax.all_gather(part, axis), value)  13.8 us
    all_gather x1, waiting for transfers between devices, body(): lax.all_gather(w_proj_bc, 'wt', axis=0, tiled=True)  12.7 us
    select_n x7, other arithmetic, turn(): jnp.where(position < mine, new, old)  10.5 us
    reduce_scatter x1, waiting for transfers between devices, body(): lax.psum_scatter(partial_out, 'head', scatter_dimension=1, tiled=True)  9.42 us
  transfers between devices with their start and end apart: 7, of which 6 were waited for; matrix products, arithmetic and copies ran while one was open for 5% of the time, Pallas kernels for 0%

commit v1 on v0

--- a/solution.py
+++ b/solution.py
@@ -7,6 +7,27 @@
 BLK = 128
 eps_value = 1e-05
 highest = lax.Precision.HIGHEST
+
+
+def in_order(blocks, dim):
+    blocks = jnp.moveaxis(blocks, 0, dim)
+    shape = blocks.shape
+    return blocks.reshape(*shape[:dim], shape[dim] * shape[dim + 1], *shape[dim + 2 :])
+
+
+def collected_by_bits(x, axis):
+    size, mine = (lax.axis_size(axis), lax.axis_index(axis))
+    blocks, bit = (x[None], 1)
+    while bit < size:
+        other = lax.ppermute(blocks, axis, [(i, i ^ bit) for i in range(size)])
+        low = mine & bit == 0
+        blocks = jnp.concatenate([jnp.where(low, blocks, other), jnp.where(low, other, blocks)])
+        bit *= 2
+    return blocks
+
+
+def doubled_up(array, axis, dim):
+    return in_order(collected_by_bits(array, axis), dim)
 
 
 def prefix(value, axis, join, neutral):
@@ -143,9 +164,7 @@
         .astype(jnp.bfloat16)
         .reshape(tokens_here, heads_here * head_size)
     )
-    partial_out = jnp.dot(
-        y_norm, lax.all_gather(w_out, "wt", axis=1, tiled=True), preferred_element_type=jnp.float32
-    )
+    partial_out = jnp.dot(y_norm, doubled_up(w_out, "wt", 1), preferred_element_type=jnp.float32)
     head_total = lax.psum_scatter(partial_out, "head", scatter_dimension=1, tiled=True)
     own_part = hidden.astype(jnp.float32)
     mixed_in = (own_part + head_total).astype(jnp.bfloat16)

time: 418 us -> 397 us (0.950)
  waiting for transfers between devices: 327 us -> 133 us
  blocking collectives: 21.3 us -> 163 us
  local copies, waits for them, and re-layouts: 5.7 us -> 20.8 us
  other arithmetic: 15.8 us -> 29.9 us
    all_gather x1, blocking collectives: 13.8 us -> 156 us  [prefix(): pieces = jax.tree.map(lambda part: lax.all_gather(part, axis), value)]
    all_gather x1, waiting for transfers between devices: 108 us -> 0.02 us  [prefix(): pieces = jax.tree.map(lambda part: lax.all_gather(part, axis), value)]
    all_gather x1 -> x0, waiting for transfers between devices: 90.1 us -> none  [body(): lax.all_gather(w_out, 'wt', axis=1, tiled=True)]
    exp x7, local copies, waits for them, and re-layouts: 0.06 us -> 8.77 us  [combine(): jnp.exp(later[0])[:, None, None] * earlier[1] + later[1]]
    concatenate x0 -> x1, other arithmetic: none -> 7.46 us  [collected_by_bits(): jnp.concatenate([jnp.where(low, blocks, other), jnp.where(low, other, blo...]
    unnamed x12 -> x21, local copies, waits for them, and re-layouts: 0.04 us -> 6.56 us
    select_n x0 -> x1, other arithmetic: none -> 5.77 us  [collected_by_bits(): jnp.where(low, blocks, other)]
  transfers between devices with their start and end apart: 7 -> 7, of which waited for: 6 -> 4; matrix products, arithmetic and copies ran while one was open for 5% -> 7% of each run, Pallas kernels for 0% -> 0%
where the time goes in v1:
time: 397 us; the launch traced here: 396 us
  blocking collectives  163 us (41%)
  waiting for transfers between devices  133 us (34%)
  other arithmetic  29.9 us (8%)
  between operations  21.8 us (5%)
  matrix products  20.9 us (5%)
  local copies, waits for them, and re-layouts  20.8 us (5%)
  starting transfers between devices  6.61 us (2%)
    all_gather x1, blocking collectives, prefix(): pieces = jax.tree.map(lambda part: lax.all_gather(part, axis), value)  156 us
    all_gather x1, waiting for transfers between devices, body(): lax.all_gather(w_proj_x, 'wt', axis=0, tiled=True)  104 us
    all_gather x1, waiting for transfers between devices, body(): lax.all_gather(w_proj_bc, 'wt', axis=0, tiled=True)  13.9 us
    reduce_scatter x1, waiting for transfers between devices, body(): lax.psum_scatter(partial_out, 'head', scatter_dimension=1, tiled=True)  12.3 us
    select_n x7, other arithmetic, turn(): jnp.where(position < mine, new, old)  10.2 us
    exp x7, local copies, waits for them, and re-layouts, combine(): jnp.exp(later[0])[:, None, None] * earlier[1] + later[1]  8.77 us
  transfers between devices with their start and end apart: 7, of which 4 were waited for; matrix products, arithmetic and copies ran while one was open for 7% of the time, Pallas kernels for 0%

profile of v1, /device:TPU:9, one launch (start us, length us, event | category | flops | bytes accessed | tf_op | source)
XLA Modules:
  0.0 396.2 jit_solution(16412527817980228813)
XLA Ops:
  6.5 0.0 all-gather.8.cloned.1.call-start
  6.6 0.7 all-gather.8.cloned.1.call-update
  7.3 0.0 all-gather.6.cloned.1.call-start
  7.3 0.7 all-gather.6.cloned.1.call-update
  8.0 0.0 all-gather.10.cloned.1.call-start
  8.8 3.4 all_gather.22
  12.2 3.6 all_gather.19
  15.8 0.2 fusion.3
  16.0 0.3 fusion.39
  16.4 0.1 multiply_bitcast_fusion
  16.5 0.1 copy.33
  16.6 0.2 reduce_window_sum.13
  16.7 0.1 copy.37
  16.8 0.6 bitcast_exponential_fusion
  17.4 0.1 copy.38
  17.5 13.9 %all-gather.8.cloned.1.call-done = bf16[2048,256]{1,0:T(8,128)(2,1)} async-done(((bf16[1024,256]{1,0:T(8,128)(2,1)}), bf16[2048,256]{1,0:T(8,128)(2,1)}) %all-gather.8.cloned.1.call-update) | async-done | bytes 1048592 | tf_op jit(solution)/shard_map/all_gather | solution.py:117
  31.4 1.6 multiply_convert_fusion.1
  33.0 104.0 %all-gather.6.cloned.1.call-done = bf16[2048,2048]{1,0:T(8,128)(2,1)} async-done(((bf16[1024,2048]{1,0:T(8,128)(2,1)}), bf16[2048,2048]{1,0:T(8,128)(2,1)}) %all-gather.6.cloned.1.call-update) | async-done | bytes 8388624 | tf_op jit(solution)/shard_map/all_gather | solution.py:116
  137.0 0.3 mul.233
  137.3 5.3 %bitcast_multiply_fusion.1 = (f32[128,2048]{1,0:T(8,128)S(1)}, bf16[128,2048]{1,0:T(8,128)(2,1)S(1)}) fusion(f32[16,8,16,128]{3,2,1,0:T(8,128)S(1)} %bitcast.115, bf16[2048,2048]{1,0:T(8,128)(2,1)} %all-gather.6.cloned.1.call-done, bf16[128,2048]{1,0:T(8,128)(2,1)S(1)} %all_gather.19, f32[2048]{0:T(1024)S(1)} %copy-done.6, f32[128]{0:T(128)S(1)} %add_rsqrt_fusion.1), kind=kOutput, calls=%fused_computation.20 | convolution fusion | flops 1076625408 | bytes 11543040 | tf_op jit(solution)/shard_map/dot_general | solution.py:122
  142.6 0.3 copy.45
  143.0 1.7 convolution_add_fusion
  144.7 0.0 reduce-scatter.2.cloned.1.call-start
  144.7 6.5 %copy.43 = bf16[2048,1024]{0,1:T(8,128)(2,1)} copy(bf16[2048,1024]{1,0:T(8,128)(2,1)} %param.26) | data formatting | bytes 8388608 | tf_op args[9]
  151.2 0.3 collective-permute-start
  151.6 156.2 %all-gather = f32[8,1,16]{2,1,0:T(1,128)} all-gather(f32[1,1,16]{2,1,0:T(1,128)S(1)} %get-tuple-element.143), channel_id=2, replica_groups=mesh['grp'=2,'seq'=4,'wt'=2,'head'=2] {'seq','wt'}, dimensions={0}, use_global_device_ids=true | all-gather | bytes 576 | tf_op jit(solution)/shard_map/all_gather | solution.py:35
  307.8 0.6 iota_compare_fusion
  308.4 0.7 broadcast_bitcast_fusion
  309.1 0.1 fusion.35
  309.2 5.8 %broadcast_select_fusion.1 = (bf16[1,2048,1024]{1,2,0:T(8,128)(2,1)}, bf16[1,2048,1024]{1,2,0:T(8,128)(2,1)}) fusion(bf16[1,2048,1024]{1,2,0:T(8,128)(2,1)} %collective-permute-done, pred[]{:T(512)S(6)} %eq.3, bf16[2048,1024]{0,1:T(8,128)(2,1)} %copy.43), kind=kLoop, calls=%fused_computation.5 | loop fusion | flops 4194304 | bytes 16777216 | tf_op jit(solution)/shard_map/jit(_where)/select_n | solution.py:24
  315.0 7.5 %pad_maximum_fusion = bf16[2,2048,1024]{1,2,0:T(8,128)(2,1)} fusion(bf16[1,2048,1024]{1,2,0:T(8,128)(2,1)} %get-tuple-element.141, bf16[1,2048,1024]{1,2,0:T(8,128)(2,1)} %get-tuple-element.140), kind=kLoop, calls=%fused_computation.3 | loop fusion | flops 4194304 | bytes 16777216 | tf_op jit(solution)/shard_map/concatenate | solution.py:24
  322.4 0.2 copy.47
  322.6 0.3 copy.44
  322.9 0.0 all-gather.10.cloned.1.call-done
  323.0 19.1 %while.15 = (s32[]{:T(128)}, f32[16,128,128]{2,1,0:T(8,128)S(1)}, s32[]{:T(128)}, f32[8,16]{1,0:T(8,128)}, f32[8,16,128,128]{3,2,1,0:T(8,128)}, /*index=5*/s32[]{:T(128)}, s32[]{:T(128)}) while((s32[]{:T(128)}, f32[16,128,128]{2,1,0:T(8,128)S(1)}, s32[]{:T(128)}, f32[8,16]{1,0:T(8,128)}, f32[8,16,128,128]{3,2,1,0:T(8,128)}, ...), condition=%wide.region_3.4_spmd.clone, body=%wide.region_2.3_spmd.clone.sunk | while | flops 1048580 | bytes 3146025 | solution.py:44
  323.0 1.3 exponential_bitcast_fusion.2
  324.2 1.5 fusion.62
  325.7 1.3 exponential_bitcast_fusion.2
  326.9 1.5 fusion.62
  328.4 1.3 exponential_bitcast_fusion.2
  329.7 1.5 fusion.62
  331.1 1.3 exponential_bitcast_fusion.2
  332.4 1.5 fusion.62
  333.9 1.3 exponential_bitcast_fusion.2
  335.1 1.5 fusion.62
  336.6 1.3 exponential_bitcast_fusion.2
  337.9 1.5 fusion.62
  339.3 1.3 exponential_bitcast_fusion.2
  340.6 1.5 fusion.62
  342.1 1.3 fusion.1
  343.4 3.2 fusion.9
  346.6 0.1 copy.42
  346.7 1.6 copy.46
  348.3 0.3 mul.247
  348.7 7.3 %fusion.16 = f32[128,2048]{1,0:T(8,128)} fusion(bf16[2048,2048]{0,1:T(8,128)(2,1)} %bitcast.107, f32[16,8,16,128]{3,2,1,0:T(8,128)S(1)} %bitcast.110, f32[128,2048]{1,0:T(8,128)S(1)} %copy.46, f32[2048]{0:T(1024)S(1)} %copy-done.4, f32[2048]{0:T(1024)S(1)} %copy-done.2, bf16[128,2048]{1,0:T(8,128)(2,1)S(1)} %get-tuple-element.155), kind=kOutput, calls=%fused_computation.32 | convolution fusion | flops 1075314688 | bytes 12075008 | tf_op jit(solution)/shard_map/dot_general | solution.py:167
  356.0 12.3 %reduce-scatter.2.cloned.1.call-done = f32[128,1024]{1,0:T(8,128)} async-done(((f32[128,2048]{1,0:T(8,128)}), f32[128,1024]{1,0:T(8,128)}) %reduce-scatter.2.cloned.1.call-update) | async-done | bytes 524304 | tf_op jit(solution)/shard_map/reduce_scatter | solution.py:168
  368.3 1.1 add_convert_fusion
  369.4 3.1 collective-permute-start.1
  372.5 3.1 collective-permute-start.2
  375.6 0.7 fusion.53
  384.1 0.7 fusion.52
  384.7 1.3 collective-permute-done.2
  386.0 0.1 pad_maximum_fusion.1
  386.1 3.6 fusion.31
  (33 shorter events, 0.2 us)
Async XLA Ops:
  6.5 2.2 copy-start.7
  6.5 2.2 copy-start.1
  6.5 5.7 %copy-start = (bf16[128,1024]{1,0:T(8,128)(2,1)S(1)}, bf16[128,1024]{1,0:T(8,128)(2,1)}, u32[]{:S(2)}) copy-start(bf16[128,1024]{1,0:T(8,128)(2,1)} %param.17) | copy-start | bytes 786436
  6.5 9.5 %copy-start.6 = (f32[2048]{0:T(1024)S(1)}, f32[2048]{0:T(1024)}, u32[]{:S(2)}) copy-start(f32[2048]{0:T(1024)} %param.18) | copy-start | bytes 24580
  6.5 9.5 %copy-start.8 = (f32[16]{0:T(128)S(1)}, f32[16]{0:T(128)}, u32[]{:S(2)}) copy-start(f32[16]{0:T(128)} %param.22) | copy-start | bytes 196
  6.5 24.9 %all-gather.8.cloned.1.call-start = ((), (), s32[]{:S(2)}) async-start(), calls=%async_computation.2 | async-start | bytes 1572864 | tf_op jit(solution)/shard_map/all_gather | solution.py:117
  7.3 129.7 %all-gather.6.cloned.1.call-start = ((), (), s32[]{:S(2)}) async-start(), calls=%async_computation.1 | async-start | bytes 12582912 | tf_op jit(solution)/shard_map/all_gather | solution.py:116
  8.0 314.9 %all-gather.10.cloned.1.call-start = ((), (), s32[]{:S(2)}) async-start(), calls=%async_computation.4 | async-start | bytes 9437184 | tf_op jit(solution)/shard_map/all_gather | solution.py:35
  144.7 163.8 %copy-start.5 = (f32[16]{0:T(128)S(1)}, f32[16]{0:T(128)}, u32[]{:S(2)}) copy-start(f32[16]{0:T(128)} %param.24) | copy-start | bytes 196
  144.7 223.6 %reduce-scatter.2.cloned.1.call-start = ((), (), s32[]{:S(2)}) async-start(), calls=%async_computation.3 | async-start | bytes 1572864 | tf_op jit(solution)/shard_map/reduce_scatter | solution.py:168
  151.2 158.0 %collective-permute-start = (bf16[1,2048,1024]{1,2,0:T(8,128)(2,1)}, bf16[1,2048,1024]{1,2,0:T(8,128)(2,1)}, u32[]{:S(2)}, u32[]{:S(2)}) collective-permute-start(bf16[1,2048,1024]{1,2,0:T(8,128)(2,1)} %bitcast.108), channel_id=1, source_target_pairs={{0,2},{2,0},{1,3},{3,1},{4,6},{6,4},{5,7},{7,5},{8,10},{10,8},{9,1... | collective-permute-start | bytes 12582920 | tf_op jit(solution)/shard_map/ppermute | solution.py:22
  343.4 5.3 %copy-start.2 = (f32[2048]{0:T(1024)S(1)}, f32[2048]{0:T(1024)}, u32[]{:S(2)}) copy-start(f32[2048]{0:T(1024)} %broadcast_bitcast_fusion) | copy-start | bytes 24580
  343.4 5.3 %copy-start.4 = (f32[2048]{0:T(1024)S(1)}, f32[2048]{0:T(1024)}, u32[]{:S(2)}) copy-start(f32[2048]{0:T(1024)} %param.25) | copy-start | bytes 24580
  348.6 26.9 %copy-start.9 = (s32[1,4]{1,0:T(1,128)S(1)}, s32[1,4]{1,0:T(1,128)}, u32[]{:S(2)}) copy-start(s32[1,4]{1,0:T(1,128)} %param.28) | copy-start | bytes 52
  348.6 35.4 %copy-start.3 = (f32[1,4]{1,0:T(1,128)S(1)}, f32[1,4]{1,0:T(1,128)}, u32[]{:S(2)}) copy-start(f32[1,4]{1,0:T(1,128)} %param.29) | copy-start | bytes 52
  369.4 15.3 %collective-permute-start.1 = (bf16[128,1024]{1,0:T(8,128)(2,1)S(1)}, bf16[128,1024]{1,0:T(8,128)(2,1)S(1)}, u32[]{:S(2)}, u32[]{:S(2)}) collective-permute-start(bf16[128,1024]{1,0:T(8,128)(2,1)S(1)} %add_convert_fusion), channel_id=1, source_target_pairs={{0,2},{2,4},{4,6},{6,8},{8,10},{10,12},{12,14},{1,3},{3,5},{5,7},{... | collective-permute-start | bytes 786440 | tf_op jit(solution)/shard_map/ppermute | solution.py:55
  372.5 13.5 %collective-permute-start.2 = (bf16[128,1024]{1,0:T(8,128)(2,1)S(1)}, bf16[128,1024]{1,0:T(8,128)(2,1)S(1)}, u32[]{:S(2)}, u32[]{:S(2)}) collective-permute-start(bf16[128,1024]{1,0:T(8,128)(2,1)S(1)} %add_convert_fusion), channel_id=1, source_target_pairs={{2,0},{4,2},{6,4},{8,6},{10,8},{12,10},{14,12},{3,1},{5,3},{7,5},{... | collective-permute-start | bytes 786440 | tf_op jit(solution)/shard_map/ppermute | solution.py:57
Sparse Core Ops, SparseCore 0:
  8.9 22.4 all-gather.7
  33.0 104.0 all-gather.5
  144.8 172.1 all-gather.9
  356.1 12.1 reduce-scatter.1
